TPU v7x, 512 devices: a whole 4x8x8 slice. The times are simulated.
512 devices in a mesh: samp: 32 (over z, x_hi, core), par: 16 (over x_lo, y).
Axes of the slice: x: 4 (x_hi: 2, x_lo: 2; x = x_hi * 2 + x_lo), y: 8, z: 8, core: 2. Of those that a mesh axis runs over, the one named last changes fastest.
Arguments:
- activations: bfloat16 [512, 2, 64, 256], P('samp'), may hold values from 0 to 2
- cotangents: bfloat16 [512, 2, 64, 256], P('samp', None, 'par'), may hold values from -0.029907227 to 0.099609375
- energies: float32 [512], P('samp'), may hold values from -3 to -1
Outputs:
- update: float32 [64, 1152], P('par')
- coeffs: float32 [512], P('samp')
All inputs are finite; a program needn't handle non-finite values.
Results may differ from a plain program's by a relative error of at most 0.0034.
Values may be sent and summed in bfloat16 or wider, within the bound.
A program may use at most 64 MiB of HBM per device.

v0:
```python
import math
import jax
import jax.numpy as jnp
from jax import lax
from jax.sharding import PartitionSpec as P

C = 64
SIDE = 16
LAYERS = 2
reg_shift = 0.1


def sample_grads(activations, cotangents):
    sample_count, layer_count, channels, site_count = activations.shape
    owned_out = cotangents.shape[2]
    field = cotangents.reshape(sample_count, layer_count, owned_out, SIDE, SIDE)
    shifted = [
        jnp.roll(field, (row_step - 1, col_step - 1), axis=(3, 4))
        for row_step in range(3)
        for col_step in range(3)
    ]
    stacked = jnp.stack(shifted, axis=3).reshape(
        sample_count, layer_count, owned_out * 9, site_count
    )
    grads = jnp.einsum("slkx,slix->slki", stacked, activations, preferred_element_type=jnp.float32)
    grads = grads.reshape(sample_count, layer_count, owned_out, 9, channels).transpose(
        0, 2, 1, 4, 3
    )
    return grads.reshape(sample_count, owned_out * layer_count * channels * 9)


def contract(left_rows, right_rows):
    return lax.dot_general(
        left_rows, right_rows, (((1,), (1,)), ((), ())), preferred_element_type=jnp.float32
    )


def solve_system(gram, dev_all, total):
    regular = gram + reg_shift * jnp.eye(total, dtype=jnp.float32)
    factor = jnp.linalg.cholesky(regular)
    forward = lax.linalg.triangular_solve(factor, dev_all[:, None], left_side=True, lower=True)
    return lax.linalg.triangular_solve(
        factor, forward, left_side=True, lower=True, transpose_a=True
    )[:, 0]


def local(activations, cotangents, energies):
    grads = sample_grads(activations, cotangents)
    local_count = grads.shape[0]
    members = lax.axis_size("samp")
    position = lax.axis_index("samp")
    total = members * local_count
    params_all = LAYERS * C * C * 9
    scale = -math.sqrt(params_all / total)
    col_sums, energy_sum = lax.psum((jnp.sum(grads, axis=0), jnp.sum(energies)), "samp")
    centered = ((grads - col_sums / total) * (1.0 / math.sqrt(params_all))).astype(jnp.bfloat16)
    deviation = energies - energy_sum / total
    partial_value = contract(centered, lax.all_gather(centered, "samp", axis=0, tiled=True))
    summed = lax.psum(partial_value, "par")
    gram, dev_column = (
        lax.all_gather(summed, "samp", axis=0, tiled=True),
        lax.all_gather(deviation[:, None], "samp", axis=0, tiled=True),
    )
    dev_all = dev_column[:, 0]
    coeffs = solve_system(gram, dev_all, total)
    local_coeffs = lax.dynamic_slice_in_dim(coeffs, position * local_count, local_count)
    term = jnp.dot(
        local_coeffs[None, :], centered.astype(jnp.float32), precision=lax.Precision.HIGHEST
    )[0]
    summed_term = lax.psum(term, "samp")
    update = scale * summed_term
    return (update.reshape(cotangents.shape[2], -1), local_coeffs)


def solution(mesh):
    return jax.shard_map(
        local,
        mesh=mesh,
        in_specs=(P("samp", None, None, None), P("samp", None, "par", None), P("samp")),
        out_specs=(P("par", None), P("samp")),
        check_vma=False,
    )
```

profile of v0, /device:TPU:8, one launch (start us, length us, event | category | flops | bytes accessed | tf_op | source)
XLA Modules:
  0.0 767.5 jit_solution(1295712559334834222)
XLA Ops:
  7.2 1.3 reshape.131
  9.5 1.0 fusion.74
  10.5 1.2 fusion.75
  11.7 1.2 fusion.72
  12.9 1.2 fusion.73
  15.0 2.5 fusion.15
  17.5 0.9 bitcast_dynamic-update-slice_fusion.2
  18.5 1.1 fusion.16
  19.6 0.6 pad_maximum_fusion.1
  20.2 0.9 fusion.20
  21.1 0.9 copy_dynamic-update-slice_fusion
  22.0 0.9 fusion.19
  22.8 1.1 fusion.17
  24.0 0.9 bitcast_dynamic-update-slice_fusion.1
  24.8 1.1 fusion.18
  25.9 6.1 reshape.132
  32.7 2.7 copy.66
  35.7 0.6 reduce_sum.22
  36.5 76.6 %psum.30 = f32[]{:T(128)} all-reduce(f32[]{:T(128)} %reduce_sum.22), channel_id=1, replica_groups=mesh['samp'=32,'par'=16] {'samp'}, use_global_device_ids=true, to_apply=%region_12.13 | all-reduce | flops 1 | bytes 8 | tf_op jit(solution)/shard_map/psum | solution.py:55
  113.1 1.3 dynamic-slice.4
  115.8 128.5 %all-reduce.2 = (f32[4608]{0:T(1024)S(1)}, f32[512]{0:T(512)S(1)}) all-reduce(f32[4608]{0:T(1024)S(1)} %reduce_sum.21, f32[512]{0:T(512)S(1)} %subtract_dynamic-update-slice_fusion), channel_id=1, replica_groups=mesh['samp'=32,'par'=16] {'samp'}, use_global_device_ids=true, to_apply=%region_1.2 | all-reduce | flops 5120 | bytes 40960 | tf_op jit(solution)/shard_map/psum | solution.py:55
  244.3 3.4 reshape.134
  247.6 0.7 multiply_convert_fusion.1
  248.4 88.7 %all-gather.4.cloned.1.call-done = bf16[512,4608]{1,0:T(8,128)(2,1)} async-done(((bf16[16,4608]{1,0:T(8,128)(2,1)}), bf16[512,4608]{1,0:T(8,128)(2,1)}) %all-gather.4.cloned.1.call-update) | async-done | bytes 4718608 | tf_op jit(solution)/shard_map/all_gather | solution.py:58
  337.2 3.7 fusion.76
  340.9 58.7 %psum.29 = f32[16,512]{1,0:T(8,128)} all-reduce(f32[16,512]{1,0:T(8,128)S(1)} %fusion.76), channel_id=1, replica_groups=mesh['samp'=32,'par'=16] {'par'}, use_global_device_ids=true, to_apply=%region_2.3 | all-reduce | flops 8192 | bytes 65536 | tf_op jit(solution)/shard_map/psum | solution.py:59
  400.1 1.1 copy.79
  401.2 2.8 convert_element_type.12
  404.1 75.9 %all-gather.6.cloned.1.call-done = f32[512,512]{1,0:T(8,128)} async-done(((f32[16,512]{1,0:T(8,128)}), f32[512,512]{1,0:T(8,128)}) %all-gather.6.cloned.1.call-update) | async-done | bytes 1048592 | tf_op jit(solution)/shard_map/all_gather | solution.py:61
  480.0 1.6 copy.68
  481.5 1.1 select_add_fusion
  482.6 1.6 copy.69
  484.4 1.0 copy-done.1
  485.4 11.7 %cholesky.103 = f32[128,128]{1,0:T(8,128)S(1)} custom-call(f32[128,128]{1,0:T(8,128)S(1)} %cholesky.263), custom_call_target="Cholesky" | custom-call | tf_op jit(solution)/shard_map/jit(cholesky)/cholesky | solution.py:40
  497.2 9.8 %custom-call.32 = f32[1,128,128]{1,2,0:T(8,128)S(1)} custom-call(f32[1,128,128]{2,1,0:T(8,128)S(1)} %get-tuple-element.55), custom_call_target="InvertDiagBlocksLowerTriangular" | custom-call | tf_op jit(solution)/shard_map/jit(cholesky)/cholesky | solution.py:40
  507.0 1.2 fusion.25
  508.2 1.3 convolution_subtract_fusion
  509.5 11.7 %cholesky.215 = f32[128,128]{1,0:T(8,128)S(1)} custom-call(f32[128,128]{1,0:T(8,128)S(1)} %cholesky.267), custom_call_target="Cholesky" | custom-call | tf_op jit(solution)/shard_map/jit(cholesky)/cholesky | solution.py:40
  521.7 10.0 %custom-call.33 = f32[1,128,128]{1,2,0:T(8,128)S(1)} custom-call(f32[1,128,128]{2,1,0:T(8,128)S(1)} %get-tuple-element.53), custom_call_target="InvertDiagBlocksLowerTriangular" | custom-call | tf_op jit(solution)/shard_map/jit(cholesky)/cholesky | solution.py:40
  532.1 1.5 convolution_subtract_fusion.1
  533.6 11.7 %cholesky.236 = f32[128,128]{1,0:T(8,128)S(1)} custom-call(f32[128,128]{1,0:T(8,128)S(1)} %cholesky.272), custom_call_target="Cholesky" | custom-call | tf_op jit(solution)/shard_map/jit(cholesky)/cholesky | solution.py:40
  545.4 9.8 %custom-call.34 = f32[1,128,128]{1,2,0:T(8,128)S(1)} custom-call(f32[1,128,128]{2,1,0:T(8,128)S(1)} %get-tuple-element.51), custom_call_target="InvertDiagBlocksLowerTriangular" | custom-call | tf_op jit(solution)/shard_map/jit(cholesky)/cholesky | solution.py:40
  555.6 1.3 convolution_subtract_fusion.2
  556.9 12.0 %cholesky.253 = f32[128,128]{1,0:T(8,128)S(1)} custom-call(f32[128,128]{1,0:T(8,128)S(1)} %convolution_subtract_fusion.2), custom_call_target="Cholesky" | custom-call | tf_op jit(solution)/shard_map/jit(cholesky)/cholesky | solution.py:40
  569.0 0.7 compare_reduce_fusion.2
  569.7 0.6 compare_reduce_fusion.3
  570.3 0.6 compare_reduce_fusion.1
  571.0 0.7 compare_reduce_fusion
  574.3 11.3 %while.1 = (s32[]{:T(128)}, f32[512,512]{0,1:T(8,128)S(1)}, s32[4,2]{0,1:T(2,128)S(1)}, f32[4,128,128]{2,1,0:T(8,128)}, s32[]{:T(128)}) while((s32[]{:T(128)}, f32[512,512]{0,1:T(8,128)S(1)}, s32[4,2]{0,1:T(2,128)S(1)}, f32[4,128,128]{2,1,0:T(8,128)}, s32[]{:T(128)}) %tuple.39), condition=%wide.while_cond, body=%wide.while_body.sunk | while | flops 2 | bytes 393829 | solution.py:42
  574.4 0.6 fusion.100
  575.0 1.4 dynamic-slice.9
  576.5 0.6 bitcast_dynamic-update-slice_fusion.4
  577.2 0.6 fusion.100
  577.8 1.4 dynamic-slice.9
  579.4 0.6 bitcast_dynamic-update-slice_fusion.4
  580.0 0.6 fusion.100
  580.6 1.4 dynamic-slice.9
  582.2 0.6 bitcast_dynamic-update-slice_fusion.4
  582.9 0.6 fusion.100
  583.5 1.4 dynamic-slice.9
  585.0 0.6 bitcast_dynamic-update-slice_fusion.4
  585.6 40.1 %custom-call.35 = f32[4,128,128]{1,2,0:T(8,128)S(1)} custom-call(f32[4,128,128]{2,1,0:T(8,128)} %get-tuple-element.9), custom_call_target="InvertDiagBlocksLowerTriangular" | custom-call | tf_op jit(solution)/shard_map/triangular_solve | solution.py:42
  629.0 130.5 %psum.31 = f32[4608]{0:T(1024)S(1)} all-reduce(f32[4608]{0:T(1024)S(1)} %convolution_reduce_fusion), channel_id=1, replica_groups=mesh['samp'=32,'par'=16] {'samp'}, use_global_device_ids=true, to_apply=%region_13.14 | all-reduce | flops 4608 | bytes 36864 | tf_op jit(solution)/shard_map/psum | solution.py:70
  759.6 0.6 reshape.144
  (89 shorter events, 9.3 us)
Async XLA Ops:
  7.2 24.9 %copy-start = (bf16[16,2,64,256]{3,2,1,0:T(8,128)(2,1)S(1)}, bf16[16,2,64,256]{3,2,1,0:T(8,128)(2,1)}, u32[]{:S(2)}) copy-start(bf16[16,2,64,256]{3,2,1,0:T(8,128)(2,1)} %param.3) | copy-start | bytes 3145732
  7.2 330.0 %all-gather.4.cloned.1.call-start = ((), (), s32[]{:S(2)}) async-start(), calls=%async_computation | async-start | bytes 4866048 | tf_op jit(solution)/shard_map/all_gather | solution.py:58
  9.5 4.6 copy-start.7
  14.5 4.0 copy-start.2
  14.5 5.1 copy-start.3
  14.5 5.1 copy-start.4
  14.5 5.1 copy-start.5
  14.5 5.1 copy-start.6
  32.0 3.7 copy-start.9
  248.4 231.6 %all-gather.6.cloned.1.call-start = ((), (), s32[]{:S(2)}) async-start(), calls=%async_computation.1 | async-start | bytes 1081344 | tf_op jit(solution)/shard_map/all_gather | solution.py:61
  484.4 1.0 copy-start.1
  628.8 131.4 %copy-start.8 = (f32[16,1]{0,1:T(1,128)}, f32[16,1]{0,1:T(1,128)S(1)}, u32[]{:S(2)}) copy-start(f32[16,1]{0,1:T(1,128)S(1)} %fusion.59) | copy-start | bytes 196
Sparse Core Ops, SparseCore 0:
  248.5 88.6 all-gather.3
  399.8 80.1 all-gather.5
where the time goes:
time: 777 us; the launch traced here: 767 us
  blocking collectives  394 us (51%)
  waiting for transfers between devices  165 us (21%)
  other arithmetic  130 us (17%)
  local copies, waits for them, and re-layouts  46.6 us (6%)
  between operations  18.8 us (2%)
  matrix products  13.2 us (2%)
    psum x2, blocking collectives, local(): lax.psum((jnp.sum(grads, axis=0), jnp.sum(energies)), 'samp')  205 us
    psum x1, blocking collectives, local(): summed_term = lax.psum(term, 'samp')  131 us
    all_gather x1, waiting for transfers between devices, local(): lax.all_gather(centered, 'samp', axis=0, tiled=True)  88.7 us
    another operation x15, other arithmetic, solve_system(): factor = jnp.linalg.cholesky(regular)  79.5 us
    all_gather x1, waiting for transfers between devices, local(): lax.all_gather(summed, 'samp', axis=0, tiled=True)  75.9 us
    psum x1, blocking collectives, local(): summed = lax.psum(partial_value, 'par')  58.7 us
    another operation x4, other arithmetic, solve_system(): lax.linalg.triangular_solve(factor, forward, left_side=True, lower=True,...  40.4 us
  transfers between devices with their start and end apart: 2, of which 2 were waited for; matrix products, arithmetic and copies ran while one was open for 1% of the time, Pallas kernels for 0%

commit v1 on v0

--- a/solution.py
+++ b/solution.py
@@ -56,7 +56,7 @@
     centered = ((grads - col_sums / total) * (1.0 / math.sqrt(params_all))).astype(jnp.bfloat16)
     deviation = energies - energy_sum / total
     partial_value = contract(centered, lax.all_gather(centered, "samp", axis=0, tiled=True))
-    summed = lax.psum(partial_value, "par")
+    summed = jnp.sum(lax.all_gather(partial_value, "par"), axis=0)
     gram, dev_column = (
         lax.all_gather(summed, "samp", axis=0, tiled=True),
         lax.all_gather(deviation[:, None], "samp", axis=0, tiled=True),

time: 777 us -> 750 us (0.965)
  blocking collectives: 394 us -> 369 us
    psum x1 -> x0, blocking collectives: 58.7 us -> none  [local(): summed = lax.psum(partial_value, 'par')]
    all_gather x0 -> x1, blocking collectives: none -> 33 us  [local(): summed = jnp.sum(lax.all_gather(partial_value, 'par'), axis=0)]
where the time goes in v1:
time: 750 us; the launch traced here: 740 us
  blocking collectives  369 us (49%)
  waiting for transfers between devices  163 us (22%)
  other arithmetic  130 us (17%)
  local copies, waits for them, and re-layouts  46.6 us (6%)
  between operations  18.8 us (3%)
  matrix products  13.2 us (2%)
    psum x2, blocking collectives, local(): lax.psum((jnp.sum(grads, axis=0), jnp.sum(energies)), 'samp')  205 us
    psum x1, blocking collectives, local(): summed_term = lax.psum(term, 'samp')  131 us
    all_gather x1, waiting for transfers between devices, local(): lax.all_gather(centered, 'samp', axis=0, tiled=True)  88.7 us
    another operation x15, other arithmetic, solve_system(): factor = jnp.linalg.cholesky(regular)  79.5 us
    all_gather x1, waiting for transfers between devices, local(): lax.all_gather(summed, 'samp', axis=0, tiled=True)  74 us
    another operation x4, other arithmetic, solve_system(): lax.linalg.triangular_solve(factor, forward, left_side=True, lower=True,...  40.4 us
    all_gather x1, blocking collectives, local(): summed = jnp.sum(lax.all_gather(partial_value, 'par'), axis=0)  33 us
  transfers between devices with their start and end apart: 2, of which 2 were waited for; matrix products, arithmetic and copies ran while one was open for 1% of the time, Pallas kernels for 0%

profile of v1, /device:TPU:8, one launch (start us, length us, event | category | flops | bytes accessed | tf_op | source)
XLA Modules:
  0.0 740.5 jit_solution(8483731953948945525)
XLA Ops:
  7.2 1.3 reshape.131
  9.5 1.0 fusion.74
  10.5 1.2 fusion.75
  11.7 1.2 fusion.72
  12.9 1.2 fusion.73
  15.0 2.5 fusion.15
  17.5 0.9 bitcast_dynamic-update-slice_fusion.2
  18.5 1.1 fusion.16
  20.2 0.9 fusion.20
  21.1 0.9 copy_dynamic-update-slice_fusion
  22.0 0.9 fusion.19
  22.8 1.1 fusion.17
  24.0 0.9 bitcast_dynamic-update-slice_fusion.1
  24.8 1.1 fusion.18
  25.9 6.1 reshape.132
  32.7 2.7 copy.64
  35.7 0.6 reduce_sum.32
  36.5 76.6 %psum.22 = f32[]{:T(128)} all-reduce(f32[]{:T(128)} %reduce_sum.32), channel_id=1, replica_groups=mesh['samp'=32,'par'=16] {'samp'}, use_global_device_ids=true, to_apply=%region_12.13 | all-reduce | flops 1 | bytes 8 | tf_op jit(solution)/shard_map/psum | solution.py:55
  113.1 1.3 dynamic-slice.4
  115.8 128.5 %all-reduce.2 = (f32[4608]{0:T(1024)S(1)}, f32[512]{0:T(512)S(1)}) all-reduce(f32[4608]{0:T(1024)S(1)} %reduce_sum.30, f32[512]{0:T(512)S(1)} %subtract_dynamic-update-slice_fusion), channel_id=1, replica_groups=mesh['samp'=32,'par'=16] {'samp'}, use_global_device_ids=true, to_apply=%region_1.2 | all-reduce | flops 5120 | bytes 40960 | tf_op jit(solution)/shard_map/psum | solution.py:55
  244.3 3.4 reshape.134
  247.6 0.7 multiply_convert_fusion.1
  248.4 88.7 %all-gather.5.cloned.1.call-done = bf16[512,4608]{1,0:T(8,128)(2,1)} async-done(((bf16[16,4608]{1,0:T(8,128)(2,1)}), bf16[512,4608]{1,0:T(8,128)(2,1)}) %all-gather.5.cloned.1.call-update) | async-done | bytes 4718608 | tf_op jit(solution)/shard_map/all_gather | solution.py:58
  337.2 3.7 fusion.76
  340.9 33.0 %all-gather = f32[256,512]{1,0:T(8,128)S(1)} all-gather(f32[16,512]{1,0:T(8,128)S(1)} %fusion.76), channel_id=2, replica_groups=mesh['samp'=32,'par'=16] {'par'}, dimensions={0}, use_global_device_ids=true | all-gather | bytes 557056 | tf_op jit(solution)/shard_map/all_gather | solution.py:59
  373.9 0.6 reduce_sum.31
  375.0 1.1 copy.77
  376.1 2.8 convert_element_type.12
  379.0 74.0 %all-gather.7.cloned.1.call-done = f32[512,512]{1,0:T(8,128)} async-done(((f32[16,512]{1,0:T(8,128)}), f32[512,512]{1,0:T(8,128)}) %all-gather.7.cloned.1.call-update) | async-done | bytes 1048592 | tf_op jit(solution)/shard_map/all_gather | solution.py:61
  452.9 1.6 copy.66
  454.5 1.1 select_add_fusion
  455.6 1.6 copy.67
  457.4 1.0 copy-done.1
  458.4 11.7 %cholesky.103 = f32[128,128]{1,0:T(8,128)S(1)} custom-call(f32[128,128]{1,0:T(8,128)S(1)} %cholesky.263), custom_call_target="Cholesky" | custom-call | tf_op jit(solution)/shard_map/jit(cholesky)/cholesky | solution.py:40
  470.1 9.8 %custom-call.32 = f32[1,128,128]{1,2,0:T(8,128)S(1)} custom-call(f32[1,128,128]{2,1,0:T(8,128)S(1)} %get-tuple-element.55), custom_call_target="InvertDiagBlocksLowerTriangular" | custom-call | tf_op jit(solution)/shard_map/jit(cholesky)/cholesky | solution.py:40
  480.0 1.2 fusion.25
  481.2 1.3 convolution_subtract_fusion
  482.5 11.7 %cholesky.215 = f32[128,128]{1,0:T(8,128)S(1)} custom-call(f32[128,128]{1,0:T(8,128)S(1)} %cholesky.267), custom_call_target="Cholesky" | custom-call | tf_op jit(solution)/shard_map/jit(cholesky)/cholesky | solution.py:40
  494.7 10.0 %custom-call.33 = f32[1,128,128]{1,2,0:T(8,128)S(1)} custom-call(f32[1,128,128]{2,1,0:T(8,128)S(1)} %get-tuple-element.53), custom_call_target="InvertDiagBlocksLowerTriangular" | custom-call | tf_op jit(solution)/shard_map/jit(cholesky)/cholesky | solution.py:40
  505.0 1.5 convolution_subtract_fusion.1
  506.6 11.7 %cholesky.236 = f32[128,128]{1,0:T(8,128)S(1)} custom-call(f32[128,128]{1,0:T(8,128)S(1)} %cholesky.272), custom_call_target="Cholesky" | custom-call | tf_op jit(solution)/shard_map/jit(cholesky)/cholesky | solution.py:40
  518.4 9.8 %custom-call.34 = f32[1,128,128]{1,2,0:T(8,128)S(1)} custom-call(f32[1,128,128]{2,1,0:T(8,128)S(1)} %get-tuple-element.51), custom_call_target="InvertDiagBlocksLowerTriangular" | custom-call | tf_op jit(solution)/shard_map/jit(cholesky)/cholesky | solution.py:40
  528.5 1.3 convolution_subtract_fusion.2
  529.9 12.0 %cholesky.253 = f32[128,128]{1,0:T(8,128)S(1)} custom-call(f32[128,128]{1,0:T(8,128)S(1)} %convolution_subtract_fusion.2), custom_call_target="Cholesky" | custom-call | tf_op jit(solution)/shard_map/jit(cholesky)/cholesky | solution.py:40
  542.0 0.7 compare_reduce_fusion.2
  542.7 0.6 compare_reduce_fusion.3
  543.3 0.6 compare_reduce_fusion.1
  543.9 0.7 compare_reduce_fusion
  547.3 11.3 %while.1 = (s32[]{:T(128)}, f32[512,512]{0,1:T(8,128)S(1)}, s32[4,2]{0,1:T(2,128)S(1)}, f32[4,128,128]{2,1,0:T(8,128)}, s32[]{:T(128)}) while((s32[]{:T(128)}, f32[512,512]{0,1:T(8,128)S(1)}, s32[4,2]{0,1:T(2,128)S(1)}, f32[4,128,128]{2,1,0:T(8,128)}, s32[]{:T(128)}) %tuple.39), condition=%wide.while_cond, body=%wide.while_body.sunk | while | flops 2 | bytes 393829 | solution.py:42
  547.4 0.6 fusion.100
  548.0 1.4 dynamic-slice.9
  549.5 0.6 bitcast_dynamic-update-slice_fusion.4
  550.2 0.6 fusion.100
  550.8 1.4 dynamic-slice.9
  552.3 0.6 bitcast_dynamic-update-slice_fusion.4
  553.0 0.6 fusion.100
  553.6 1.4 dynamic-slice.9
  555.1 0.6 bitcast_dynamic-update-slice_fusion.4
  555.8 0.6 fusion.100
  556.4 1.4 dynamic-slice.9
  558.0 0.6 bitcast_dynamic-update-slice_fusion.4
  558.6 40.1 %custom-call.35 = f32[4,128,128]{1,2,0:T(8,128)S(1)} custom-call(f32[4,128,128]{2,1,0:T(8,128)} %get-tuple-element.9), custom_call_target="InvertDiagBlocksLowerTriangular" | custom-call | tf_op jit(solution)/shard_map/triangular_solve | solution.py:42
  602.0 130.5 %psum.23 = f32[4608]{0:T(1024)S(1)} all-reduce(f32[4608]{0:T(1024)S(1)} %convolution_reduce_fusion), channel_id=1, replica_groups=mesh['samp'=32,'par'=16] {'samp'}, use_global_device_ids=true, to_apply=%region_13.14 | all-reduce | flops 4608 | bytes 36864 | tf_op jit(solution)/shard_map/psum | solution.py:70
  732.6 0.6 reshape.144
  (90 shorter events, 9.8 us)
Async XLA Ops:
  7.2 24.9 %copy-start = (bf16[16,2,64,256]{3,2,1,0:T(8,128)(2,1)S(1)}, bf16[16,2,64,256]{3,2,1,0:T(8,128)(2,1)}, u32[]{:S(2)}) copy-start(bf16[16,2,64,256]{3,2,1,0:T(8,128)(2,1)} %param.3) | copy-start | bytes 3145732
  7.2 330.0 %all-gather.5.cloned.1.call-start = ((), (), s32[]{:S(2)}) async-start(), calls=%async_computation | async-start | bytes 4866048 | tf_op jit(solution)/shard_map/all_gather | solution.py:58
  9.5 4.6 copy-start.7
  14.5 4.0 copy-start.2
  14.5 5.1 copy-start.3
  14.5 5.1 copy-start.4
  14.5 5.1 copy-start.5
  14.5 5.1 copy-start.6
  32.0 3.7 copy-start.9
  248.4 204.6 %all-gather.7.cloned.1.call-start = ((), (), s32[]{:S(2)}) async-start(), calls=%async_computation.1 | async-start | bytes 1081344 | tf_op jit(solution)/shard_map/all_gather | solution.py:61
  457.4 1.0 copy-start.1
  601.8 131.4 %copy-start.8 = (f32[16,1]{0,1:T(1,128)}, f32[16,1]{0,1:T(1,128)S(1)}, u32[]{:S(2)}) copy-start(f32[16,1]{0,1:T(1,128)S(1)} %fusion.59) | copy-start | bytes 196
Sparse Core Ops, SparseCore 0:
  248.5 88.6 all-gather.4
  374.7 78.2 all-gather.6
